TPU v7x, 1024 devices: a whole 8x8x8 slice. The times are simulated.
1024 devices in a mesh: dp: 64 (over x, z), tensor: 8 (over y), side: 2 (over core).
Axes of the slice: x: 8, y: 8, z: 8, core: 2. Of those that a mesh axis runs over, the one named last changes fastest.
Arguments:
- tokens: bfloat16 [8192, 4096], P('dp', ('tensor', 'side')), may hold values from -6 to 6
- gain: bfloat16 [4096], P(('tensor', 'side')), may hold values from 0.25 to 1.75
- router: bfloat16 [4096, 128], P(('tensor', 'side'))
- routes: int32 [8192, 8], P('dp'), may hold values from 0 to 127, as said below
- w_gate: bfloat16 [128, 4096, 768], P(('dp', 'side'), None, 'tensor'), may hold values from -0.09375 to 0.09375
- w_up: bfloat16 [128, 4096, 768], P(('dp', 'side'), None, 'tensor'), may hold values from -0.09375 to 0.09375
- w_down: bfloat16 [128, 768, 4096], P(('dp', 'side'), 'tensor'), may hold values from -0.21875 to 0.21875
Outputs:
- mixed: bfloat16 [8192, 4096], P('dp', ('tensor', 'side'))
Inputs may be any that keep to these rules, and one draw needn't show every extreme that they name: `routes`: each row names 8 different experts. In each aligned block of 128 rows (the tokens of one dp index) no expert is named by more than 10 rows, and some expert is named by exactly 10.
All inputs are finite; a program needn't handle non-finite values.
Results may differ from a plain program's by a relative error of at most 0.02.
Values may be sent and summed in bfloat16 or wider, within the bound.
A program may use at most 64 MiB of HBM per device.

v0:
```python
import jax
import jax.numpy as jnp
from jax import lax
from jax.sharding import PartitionSpec as P


def body(tokens, gain, router, routes, w_gate, w_up, w_down):
    rows_here, feats = tokens.shape
    top = routes.shape[1]
    n_dp = lax.axis_size("dp")
    n_side = lax.axis_size("side")
    n_tensor = lax.axis_size("tensor")
    experts = n_dp * n_side
    slots = min(rows_here, max(2, rows_here * top * 5 // (experts * 4)))
    width = feats * n_side * n_tensor
    xf = tokens.astype(jnp.float32)
    gf = gain.astype(jnp.float32)
    router_f = router.astype(jnp.float32)
    square = jnp.sum(xf * xf, axis=1)
    total = lax.psum(square, ("tensor", "side"))
    rinv = lax.rsqrt(total / width + 1e-06)
    scaled = xf * rinv[:, None] * gf
    logits = lax.psum(
        jnp.dot(scaled, router_f, precision=lax.Precision.HIGHEST), ("tensor", "side")
    )
    normed = (xf * rinv[:, None] * gf).astype(jnp.bfloat16)
    expert_ids = jnp.arange(experts, dtype=jnp.int32)
    onehot = routes[:, :, None] == expert_ids[None, None, :]
    picked = jnp.sum(jnp.where(onehot, logits[:, None, :], 0.0), axis=-1)
    weights = jax.nn.softmax(picked, axis=-1)
    counts = jnp.sum(onehot.astype(jnp.int32), axis=1)
    before = jnp.cumsum(counts, axis=0) - counts
    slot = jnp.sum(jnp.where(onehot, before[:, None, :], 0), axis=-1)
    position = routes * slots + slot
    places = jnp.arange(experts * slots, dtype=jnp.int32)
    matches = position[:, :, None] == places[None, None, :]
    chosen = jnp.sum(matches.astype(jnp.float32), axis=1).astype(jnp.bfloat16)
    send = lax.dot_general(
        chosen, normed, (((0,), (0,)), ((), ())), preferred_element_type=jnp.float32
    ).astype(jnp.bfloat16)
    send = send.reshape(n_dp, n_side, slots, feats)
    paired = lax.all_to_all(send, "side", split_axis=1, concat_axis=3, tiled=True)
    arrived = lax.all_to_all(
        paired.reshape(n_dp, slots, feats * n_side), "dp", split_axis=0, concat_axis=0, tiled=True
    )
    rows_in = arrived.reshape(n_dp * slots, feats * n_side)
    gate_w = w_gate[0]
    up_w = w_up[0]
    down_w = w_down[0]
    piece = lax.all_gather(rows_in, "tensor", axis=1, tiled=True)
    gate = jnp.dot(piece, gate_w, preferred_element_type=jnp.float32)
    upper = jnp.dot(piece, up_w, preferred_element_type=jnp.float32)
    hidden = (jax.nn.silu(gate) * upper).astype(jnp.bfloat16)
    summed = lax.psum_scatter(
        lax.dot_general(
            down_w, hidden, (((0,), (1,)), ((), ())), preferred_element_type=jnp.float32
        ).astype(jnp.bfloat16),
        "tensor",
        scatter_dimension=0,
        tiled=True,
    )
    back = summed.reshape(n_side, feats, n_dp, slots)
    returned = lax.all_to_all(
        lax.all_to_all(back, "dp", split_axis=2, concat_axis=2, tiled=True),
        "side",
        split_axis=0,
        concat_axis=0,
        tiled=True,
    )
    combine = jnp.sum(jnp.where(matches, weights[:, :, None], 0.0), axis=1)
    combine = combine.reshape(rows_here, n_dp, n_side, slots)
    mixed = jnp.einsum(
        "tesc,sfec->tf", combine, returned.astype(jnp.float32), precision=lax.Precision.HIGHEST
    )
    return mixed.astype(jnp.bfloat16)


def solution(mesh):
    placed = (
        P("dp", ("tensor", "side")),
        P(("tensor", "side")),
        P(("tensor", "side"), None),
        P("dp", None),
        P(("dp", "side"), None, "tensor"),
        P(("dp", "side"), None, "tensor"),
        P(("dp", "side"), "tensor", None),
    )
    return jax.shard_map(
        body, mesh=mesh, in_specs=placed, out_specs=P("dp", ("tensor", "side")), check_vma=False
    )
```

profile of v0, /device:TPU:1, one launch (start us, length us, event | category | flops | bytes accessed | tf_op | source)
XLA Modules:
  0.0 408.7 jit_solution(12628217592412183740)
XLA Ops:
  6.5 1.0 fusion.16
  7.6 37.1 %psum.14 = f32[128]{0:T(128)S(1)} all-reduce(f32[128]{0:T(128)S(1)} %fusion.16), channel_id=1, replica_groups=mesh['dp'=64,'tensor'=8,'side'=2] {'tensor','side'}, use_global_device_ids=true, to_apply=%region_4.5 | all-reduce | flops 128 | bytes 1024 | tf_op jit(solution)/shard_map/psum | solution.py:20
  45.3 1.8 fusion.19
  47.1 0.8 copy.39
  48.3 2.4 select_reduce_fusion.2
  50.8 0.7 multiply_add_fusion
  51.6 106.0 %all-reduce.2.cloned.1.call-done = f32[128,128]{1,0:T(8,128)} async-done(((f32[128,128]{1,0:T(8,128)}), f32[128,128]{1,0:T(8,128)}) %all-reduce.2.cloned.1.call-update) | async-done | bytes 65552 | tf_op jit(solution)/shard_map/psum | solution.py:23
  157.6 1.2 select_reduce_fusion.1
  159.1 3.4 select_reduce_fusion
  162.6 1.2 convolution_convert_fusion.1
  164.4 4.7 %all_to_all.30 = bf16[64,2,10,256]{3,0,2,1:T(8,128)(2,1)S(1)} all-to-all(bf16[64,2,10,256]{3,0,2,1:T(8,128)(2,1)S(1)} %copy.46), channel_id=1, replica_groups=mesh['dp'=64,'tensor'=8,'side'=2] {'side'}, dimensions={1} | all-to-all | bytes 1310720 | tf_op jit(solution)/shard_map/all_to_all | solution.py:42
  170.2 38.7 %all_to_all.31 = bf16[64,10,512]{2,1,0:T(8,128)(2,1)S(1)} all-to-all(bf16[64,10,512]{2,1,0:T(8,128)(2,1)S(1)} %reshape.71), channel_id=1, replica_groups=mesh['dp'=64,'tensor'=8,'side'=2] {'dp'}, dimensions={0} | all-to-all | bytes 1310720 | tf_op jit(solution)/shard_map/all_to_all | solution.py:43
  208.9 1.1 reshape.68
  210.3 64.6 %all-gather.2.cloned.1.call-done = bf16[640,4096]{1,0:T(8,128)(2,1)} async-done(((bf16[640,512]{1,0:T(8,128)(2,1)}), bf16[640,4096]{1,0:T(8,128)(2,1)}) %all-gather.2.cloned.1.call-update) | async-done | bytes 5242896 | tf_op jit(solution)/shard_map/all_gather | solution.py:50
  274.9 4.4 %fusion.6 = f32[640,96]{0,1:T(8,128)S(1)} fusion(bf16[640,4096]{1,0:T(8,128)(2,1)} %all-gather.2.cloned.1.call-done, bf16[1,4096,96]{1,2,0:T(8,128)(2,1)} %param.11), kind=kOutput, calls=%fused_computation.12 | convolution fusion | flops 503316480 | bytes 6275072 | tf_op jit(solution)/shard_map/dot_general | solution.py:51
  279.3 8.6 %fusion = bf16[4096,640]{0,1:T(8,128)(2,1)} fusion(bf16[640,4096]{1,0:T(8,128)(2,1)} %all-gather.2.cloned.1.call-done, bf16[1,96,4096]{2,1,0:T(8,128)(2,1)S(1)} %copy-done, bf16[1,4096,96]{1,2,0:T(8,128)(2,1)S(1)} %copy-done.1, f32[640,96]{0,1:T(8,128)S(1)} %fusion.6), kind=kOutput, calls=%fused_computation.1 | convolution fusion | flops 1009623040 | bytes 12304384 | tf_op jit(solution)/shard_map/dot_general | solution.py:55
  287.9 70.0 %reduce-scatter.2.cloned.1.call-done = bf16[512,640]{0,1:T(8,128)(2,1)} async-done(((bf16[4096,640]{0,1:T(8,128)(2,1)}), bf16[512,640]{0,1:T(8,128)(2,1)}) %reduce-scatter.2.cloned.1.call-update) | async-done | bytes 655376 | tf_op jit(solution)/shard_map/reduce_scatter | solution.py:54
  358.0 2.7 reshape.69
  360.7 13.7 %all-to-all-start.2 = ((bf16[2,256,64,10]{1,0,3,2:T(2,128)(2,1)}), bf16[2,256,64,10]{1,0,3,2:T(2,128)(2,1)S(1)}, u32[]{:S(2)}, u32[]{:S(2)}) async-start(bf16[2,256,64,10]{1,0,3,2:T(2,128)(2,1)} %reshape.69), calls=%async_computation.3 | async-start | bytes 1310720 | tf_op jit(solution)/shard_map/all_to_all | solution.py:64
  374.4 1.1 copy.45
  375.5 1.2 reshape.65
  376.6 16.3 %all-to-all-done.2 = bf16[2,256,64,10]{1,0,3,2:T(2,128)(2,1)S(1)} async-done(((bf16[2,256,64,10]{1,0,3,2:T(2,128)(2,1)}), bf16[2,256,64,10]{1,0,3,2:T(2,128)(2,1)S(1)}, u32[]{:S(2)}, u32[]{:S(2)}) %all-to-all-start.2) | async-done | bytes 655392 | tf_op jit(solution)/shard_map/all_to_all | solution.py:64
  393.1 7.5 %all_to_all.32 = bf16[2,256,64,10]{1,2,3,0:T(8,128)(2,1)S(1)} all-to-all(bf16[2,256,64,10]{1,2,3,0:T(8,128)(2,1)S(1)} %copy.49), channel_id=1, replica_groups=mesh['dp'=64,'tensor'=8,'side'=2] {'side'}, dimensions={0} | all-to-all | bytes 1310720 | tf_op jit(solution)/shard_map/all_to_all | solution.py:63
  400.6 1.6 fusion.2
  (27 shorter events, 3.7 us)
Async XLA Ops:
  6.5 272.8 %copy-start = (bf16[1,96,4096]{2,1,0:T(8,128)(2,1)S(1)}, bf16[1,96,4096]{2,1,0:T(8,128)(2,1)}, u32[]{:S(2)}) copy-start(bf16[1,96,4096]{2,1,0:T(8,128)(2,1)} %param.13) | copy-start | bytes 2359300
  6.5 151.1 %all-reduce.2.cloned.1.call-start = ((), (), s32[]{:S(2)}) async-start(), calls=%async_computation.5 | async-start | bytes 131072 | tf_op jit(solution)/shard_map/psum | solution.py:23
  47.1 227.8 %all-gather.2.cloned.1.call-start = ((), (), s32[]{:S(2)}) async-start(), calls=%async_computation.6 | async-start | bytes 5898240 | tf_op jit(solution)/shard_map/all_gather | solution.py:50
  208.9 70.4 %copy-start.1 = (bf16[1,4096,96]{1,2,0:T(8,128)(2,1)S(1)}, bf16[1,4096,96]{1,2,0:T(8,128)(2,1)}, u32[]{:S(2)}) copy-start(bf16[1,4096,96]{1,2,0:T(8,128)(2,1)} %param.12) | copy-start | bytes 2359300
  210.1 147.9 %reduce-scatter.2.cloned.1.call-start = ((), (), s32[]{:S(2)}) async-start(), calls=%async_computation.7 | async-start | bytes 5898240 | tf_op jit(solution)/shard_map/reduce_scatter | solution.py:54
  360.7 32.3 %all-to-all-start.2 = ((bf16[2,256,64,10]{1,0,3,2:T(2,128)(2,1)}), bf16[2,256,64,10]{1,0,3,2:T(2,128)(2,1)S(1)}, u32[]{:S(2)}, u32[]{:S(2)}) async-start(bf16[2,256,64,10]{1,0,3,2:T(2,128)(2,1)} %reshape.69), calls=%async_computation.3 | async-start | bytes 1310720 | tf_op jit(solution)/shard_map/all_to_all | solution.py:64
Sparse Core Ops, SparseCore 0:
  47.2 110.3 all-reduce.1
  210.2 64.7 all-gather.1
  288.1 69.8 reduce-scatter.1
where the time goes:
time: 410 us; the launch traced here: 409 us
  waiting for transfers between devices  257 us (63%)
  blocking collectives  88 us (21%)
  matrix products  17.6 us (4%)
  starting transfers between devices  14 us (3%)
  between operations  13.2 us (3%)
  other arithmetic  9.96 us (2%)
  local copies, waits for them, and re-layouts  8.9 us (2%)
    psum x1, waiting for transfers between devices, body(): lax.psum(jnp.dot(scaled, router_f, precision=lax.Precision.HIGHEST), ('te...  106 us
    reduce_scatter x1, waiting for transfers between devices, body(): lax.psum_scatter(lax.dot_general(down_w, hidden, (((0,), (1,)), ((), ()))...  70 us
    all_gather x1, waiting for transfers between devices, body(): piece = lax.all_gather(rows_in, 'tensor', axis=1, tiled=True)  64.6 us
    all_to_all x1, blocking collectives, body(): lax.all_to_all(paired.reshape(n_dp, slots, feats * n_side), 'dp', split_a...  38.7 us
    psum x1, blocking collectives, body(): total = lax.psum(square, ('tensor', 'side'))  37.1 us
    all_to_all x1, waiting for transfers between devices, body(): lax.all_to_all(back, 'dp', split_axis=2, concat_axis=2, tiled=True)  16.3 us
    all_to_all x1, starting transfers between devices, body(): lax.all_to_all(back, 'dp', split_axis=2, concat_axis=2, tiled=True)  13.7 us
    dot_general x1, matrix products, body(): lax.dot_general(down_w, hidden, (((0,), (1,)), ((), ())), preferred_eleme...  8.59 us
  transfers between devices with their start and end apart: 4, of which 4 were waited for; matrix products, arithmetic and copies ran while one was open for 2% of the time, Pallas kernels for 0%

commit v1 on v0

v1 whole, which is shorter than its diff:
```python
import functools

import jax
import jax.numpy as jnp
from jax import lax
from jax.experimental import pallas as pl
from jax.experimental.pallas import tpu as pltpu
from jax.sharding import PartitionSpec as P

MESH = pl.DeviceIdType.MESH
BF = jnp.bfloat16
F32 = jnp.float32
LANE = 128
HIGH = lax.Precision.HIGHEST
NT = (((1,), (1,)), ((), ()))
TN = (((0,), (0,)), ((), ()))


def dot(a, b, dims=(((1,), (0,)), ((), ())), precision=None):
    return lax.dot_general(a, b, dims, precision=precision, preferred_element_type=F32)


def split_slots(slots):
    return ((0, slots),)


def plane_rows(count, chunks):
    return -(-count * chunks // 16) * 16


def kernel(cfg, *refs):
    n_dp, n_t, slots, groups, toks, feats, experts, top, hid_n = cfg
    it = iter(refs)
    take = lambda n: [next(it) for _ in range(n)]
    tokens, gain, router, routes, w_gate, w_up, w_down, out = take(8)
    xtok, rt, gn, chosen, tmp, lp, lr, lg, ss, wt, wdb, ct, mixs, mixr = take(14)
    ng = len(groups)
    send, recv, send2, recv2, ag, hid, acc, oacc = [take(ng) for _ in range(8)]
    pair_s, pair_r, wd_s, wd_r, lp_s, lp_r, lg_s, lg_r, mix_s, mix_r = take(10)
    dis_s, dis_r, ret_s, ret_r, ss_s, ss_r, ag_s, ag_r, hid_s, hid_r = take(10)

    d, t, s = lax.axis_index("dp"), lax.axis_index("tensor"), lax.axis_index("side")
    nz = 8 if n_dp % 8 == 0 else n_dp
    nx = n_dp // nz
    chunks = 2 * feats // LANE
    per_half = feats // LANE
    piece = toks // n_t
    other = 1 - s

    def dp_peer(i):
        return lax.rem(d // nz + i // nz, nx) * nz + lax.rem(d % nz + i % nz, nz)

    def t_peer(i):
        return lax.rem(t + i, n_t)

    def rcopy(src, dst, ssem, rsem, dev):
        return pltpu.make_async_remote_copy(
            src_ref=src, dst_ref=dst, send_sem=ssem, recv_sem=rsem, device_id=dev, device_id_type=MESH
        )

    def wait_bytes(ref, sem):
        pltpu.make_async_copy(ref, ref, sem).wait()

    barrier = pltpu.get_barrier_semaphore()
    pl.semaphore_signal(barrier, inc=1, device_id=(d, t, other), device_id_type=MESH)

    def greet_t(i, carry):
        pl.semaphore_signal(barrier, inc=1, device_id=(d, t_peer(i), s), device_id_type=MESH)
        return carry

    def greet_dp(i, carry):
        pl.semaphore_signal(barrier, inc=1, device_id=(dp_peer(i), t, s), device_id_type=MESH)
        return carry

    lax.fori_loop(1, n_t, greet_t, 0)
    lax.fori_loop(1, n_dp, greet_dp, 0)

    e_ids = lax.broadcasted_iota(jnp.int32, (toks, experts), 1)
    routes_v = routes[...]
    onehot = jnp.zeros((toks, experts), F32)
    for k in range(top):
        onehot = onehot + jnp.where(routes_v[:, k : k + 1] == e_ids, 1.0, 0.0)
    lower = jnp.where(
        lax.broadcasted_iota(jnp.int32, (toks, toks), 1) < lax.broadcasted_iota(jnp.int32, (toks, toks), 0), 1.0, 0.0
    )
    before = dot(lower.astype(BF), onehot.astype(BF))
    taken = (onehot * (before + 1.0)).astype(BF)

    rows = slots * n_dp
    r_of = lax.broadcasted_iota(jnp.int32, (rows, experts), 0)
    expand = jnp.where(
        lax.broadcasted_iota(jnp.int32, (rows, experts), 1) == 2 * (r_of % n_dp) + s, 1.0, 0.0
    ).astype(BF)
    slot_of = lax.broadcasted_iota(jnp.int32, (rows, toks), 0) // n_dp + 1
    chosen[...] = jnp.where(dot(expand, taken, NT) == slot_of.astype(F32), 1.0, 0.0).astype(BF)
    gn[s] = jnp.broadcast_to(gain[...].astype(F32), (8, feats))
    xtok[s] = tokens[...]
    rt[s] = router[...]
    tmp[...] = jnp.zeros_like(tmp)

    pl.semaphore_wait(barrier, 1 + (n_t - 1) + (n_dp - 1))

    pairs = [
        rcopy(ref, ref, pair_s.at[i], pair_r.at[i], (d, t, other))
        for i, ref in enumerate((xtok.at[s], rt.at[s], gn.at[s]))
    ]
    for c in pairs:
        c.start()

    def wd_send(i, carry):
        p = t_peer(i)
        cols = pl.ds(pl.multiple_of(p * 2 * feats, 2 * feats), 2 * feats)
        rcopy(w_down.at[0, :, cols], wdb.at[t], wd_s, wd_r, (d, p, s)).start()
        return carry

    lax.fori_loop(1, n_t, wd_send, 0)
    wdb[t] = w_down[0, :, pl.ds(pl.multiple_of(t * 2 * feats, 2 * feats), 2 * feats)]

    def pack(value_of, g, dst):
        s0, ns = groups[g]
        pr = plane_rows(ns, chunks)
        for c in range(chunks):
            v = value_of(c)
            for q in range(ns):
                tmp[pl.ds(c * ns + q, n_dp, stride=pr), :] = v[q * n_dp : (q + 1) * n_dp]
        dst[...] = tmp[: n_dp * pr].astype(BF)

    def exchange(g, src, dst, ssem, rsem):
        pr = plane_rows(groups[g][1], chunks)

        def plane(i):
            return pl.ds(pl.multiple_of(i * pr, pr), pr)

        def one(i, carry):
            p = dp_peer(i)
            rcopy(src.at[plane(p)], dst.at[plane(d)], ssem, rsem, (p, t, s)).start()
            return carry

        lax.fori_loop(1, n_dp, one, 0)
        dst[plane(d), :] = src[plane(d), :]

    def exchange_wait(g, dst, sem):
        pr = plane_rows(groups[g][1], chunks)
        wait_bytes(dst.at[pl.ds(0, (n_dp - 1) * pr)], sem)

    pairs[0].wait_recv()
    for g, (s0, ns) in enumerate(groups):
        sel = chosen[s0 * n_dp : (s0 + ns) * n_dp]
        halves = [dot(sel, xtok[h]) for h in range(2)]
        pack(lambda c: halves[c // per_half][:, (c % per_half) * LANE : (c % per_half + 1) * LANE], g, send[g])
        exchange(g, send[g], recv[g], dis_s.at[g], dis_r.at[g])

    for c in pairs[1:]:
        c.wait_recv()
    part = jnp.zeros((toks, experts), F32)
    sq = jnp.zeros((toks, 1), F32)
    for h in range(2):
        xf = xtok[h].astype(F32)
        sq = sq + jnp.sum(xf * xf, axis=1, keepdims=True)
        part = part + dot(xf * gn[h][0:1], rt[h].astype(F32), precision=HIGH)
    for j in range(n_t):
        lp[j, 0] = part[j * piece : (j + 1) * piece]
        lp[j, 1] = jnp.broadcast_to(sq[j * piece : (j + 1) * piece], (piece, experts))

    def lp_send(i, carry):
        p = t_peer(i)
        rcopy(lp.at[p], lr.at[t], lp_s, lp_r, (d, p, s)).start()
        return carry

    lax.fori_loop(1, n_t, lp_send, 0)
    lr[t] = lp[t]

    eye = jnp.where(
        lax.broadcasted_iota(jnp.int32, (hid_n, hid_n), 0) == lax.broadcasted_iota(jnp.int32, (hid_n, hid_n), 1), 1.0, 0.0
    ).astype(BF)

    def turn(j, carry):
        for h in range(2):
            k0 = pl.ds(pl.multiple_of(j * 2 * feats + h * feats, feats), feats)
            wt[j, h, 0:hid_n] = dot(eye, w_gate[0, k0, :], NT).astype(BF)
            wt[j, h, hid_n : 2 * hid_n] = dot(eye, w_up[0, k0, :], NT).astype(BF)
        return carry

    lax.fori_loop(0, n_t, turn, 0)

    wait_bytes(lr.at[pl.ds(0, n_t - 1)], lp_r)
    tot = lr[0]
    for j in range(1, n_t):
        tot = tot + lr[j]
    width = 2 * feats * n_t
    lg[t] = tot[0] * lax.rsqrt(tot[1] / width + 1e-06)

    def lg_send(i, carry):
        rcopy(lg.at[t], lg.at[t], lg_s, lg_r, (d, t_peer(i), s)).start()
        return carry

    lax.fori_loop(1, n_t, lg_send, 0)

    right, left = t_peer(1), t_peer(n_t - 1)
    hops = n_t // 2

    def ring(ref_of, ssem, rsem, halves, hop, direction, h):
        origin = t_peer(n_t - (hop - 1)) if direction == 0 else t_peer(hop - 1)
        ref = ref_of(origin, h)
        k = (direction * hops + hop - 1) * halves + h
        return rcopy(ref, ref, ssem.at[k], rsem.at[k], (d, right if direction == 0 else left, s))

    def arrived(ref_of, ssem, rsem, halves, hop, direction, h):
        origin = t_peer(n_t - hop) if direction == 0 else t_peer(hop)
        ref = ref_of(origin, h)
        k = (direction * hops + hop - 1) * halves + h
        rcopy(ref, ref, ssem.at[k], rsem.at[k], (d, right if direction == 0 else left, s)).wait_recv()
        return origin

    def legs(hop):
        if hop < hops:
            return [(h, direction) for h in range(2) for direction in range(2)]
        return [(0, 0), (1, 1)]

    def unpack(src, g, use):
        s0, ns = groups[g]
        pr = plane_rows(ns, chunks)
        tmp[: n_dp * pr] = src[...].astype(F32)
        for q in range(ns):
            use(q, [tmp[pl.ds(c * ns + q, n_dp, stride=pr), :] for c in range(chunks)])

    for g, (s0, ns) in enumerate(groups):
        n_rows = ns * n_dp
        exchange_wait(g, recv[g], dis_r.at[g])
        squares = []

        def scale(q, cols):
            squares.append(sum(v * v for v in cols))
            for c, v in enumerate(cols):
                h, l0 = c // per_half, (c % per_half) * LANE
                ag[g][t, h, q * n_dp : (q + 1) * n_dp, l0 : l0 + LANE] = (v * gn[h][0:1, l0 : l0 + LANE]).astype(BF)

        unpack(recv[g], g, scale)
        ref_of = lambda o, h, g=g: ag[g].at[o, h]
        for h, direction in legs(1) if hops > 1 else [(0, 0), (1, 1)]:
            ring(ref_of, ag_s.at[g], ag_r.at[g], 2, 1, direction, h).start()
        ones = jnp.ones((8, LANE), F32)
        cols = pl.ds(s0 * n_dp, n_rows)
        for q in range(ns):
            ss[t, :, (s0 + q) * n_dp : (s0 + q + 1) * n_dp] = dot(ones, squares[q], NT, precision=HIGH)

        def ss_send(i, carry):
            rcopy(ss.at[t, :, cols], ss.at[t, :, cols], ss_s.at[g], ss_r.at[g], (d, t_peer(i), s)).start()
            return carry

        lax.fori_loop(1, n_t, ss_send, 0)
        acc[g][...] = dot(wt[t, 0], ag[g][t, 0], NT) + dot(wt[t, 1], ag[g][t, 1], NT)

    wait_bytes(lg.at[pl.ds(0, n_t - 1)], lg_r)
    logits = jnp.concatenate([lg[j] for j in range(n_t)], axis=0)
    masked = jnp.where(onehot > 0.0, logits, -jnp.inf)
    ex = jnp.exp(masked - jnp.max(masked, axis=1, keepdims=True))
    weights = ex / jnp.sum(ex, axis=1, keepdims=True)
    r_of = lax.broadcasted_iota(jnp.int32, (experts, rows), 1)
    expand_t = jnp.where(
        lax.broadcasted_iota(jnp.int32, (experts, rows), 0) == 2 * (r_of % n_dp) + s, 1.0, 0.0
    ).astype(BF)
    slot_of = lax.broadcasted_iota(jnp.int32, (toks, rows), 1) // n_dp + 1
    mine = dot(taken, expand_t) == slot_of.astype(F32)
    w_hi = weights.astype(BF)
    w_lo = (weights - w_hi.astype(F32)).astype(BF)
    ct[0] = jnp.where(mine, dot(w_hi, expand_t), 0.0).astype(BF)
    ct[1] = jnp.where(mine, dot(w_lo, expand_t), 0.0).astype(BF)
    wait_bytes(wdb.at[pl.ds(0, n_t - 1)], wd_r)

    for g, (s0, ns) in enumerate(groups):
        n_rows = ns * n_dp
        ref_of = lambda o, h, g=g: ag[g].at[o, h]
        for hop in range(1, hops + 1):
            coming = legs(hop)
            going = legs(hop + 1) if hop < hops else []
            for h, direction in coming:
                origin = arrived(ref_of, ag_s.at[g], ag_r.at[g], 2, hop, direction, h)
                if (h, direction) in going:
                    ring(ref_of, ag_s.at[g], ag_r.at[g], 2, hop + 1, direction, h).start()
                acc[g][...] += dot(wt[origin, h], ag[g][origin, h], NT)
        if g == 0:
            pass
        cols = slice(s0 * n_dp, (s0 + ns) * n_dp)
        wait_bytes(ss.at[pl.ds(0, n_t - 1), :, pl.ds(s0 * n_dp, n_rows)], ss_r.at[g])
        total = ss[0, 0:1, cols]
        for j in range(1, n_t):
            total = total + ss[j, 0:1, cols]
        rinv = lax.rsqrt(total / width + 1e-06)
        gate = acc[g][0:hid_n] * rinv
        hid[g][t] = (gate * jax.nn.sigmoid(gate) * (acc[g][hid_n : 2 * hid_n] * rinv)).astype(BF)

        half = hid_n // 2

        def hid_ref(o, h, g=g):
            return hid[g].at[o] if h is None else hid[g].at[o, pl.ds(h * half, half)]

        def hid_legs(hop):
            return [(None, 0), (None, 1)] if hop < hops else [(0, 0), (1, 1)]

        def hid_copy(hop, direction, h, incoming):
            step = hop if incoming else hop - 1
            origin = t_peer((n_t - step) % n_t) if direction == 0 else t_peer(step)
            ref = hid_ref(origin, h)
            k = direction * hops + hop - 1
            return origin, rcopy(
                ref, ref, hid_s.at[g, k], hid_r.at[g, k], (d, right if direction == 0 else left, s)
            )

        for h, direction in hid_legs(1):
            hid_copy(1, direction, h, False)[1].start()
        oacc[g][...] = dot(hid[g][t], wdb[t], TN)
        for hop in range(1, hops + 1):
            got = []
            for h, direction in hid_legs(hop):
                origin, c = hid_copy(hop, direction, h, True)
                c.wait_recv()
                got.append(origin)
                if hop < hops:
                    nh = None if hop + 1 < hops else direction
                    hid_copy(hop + 1, direction, nh, False)[1].start()
            for origin in got if hop < hops else got[:1]:
                oacc[g][...] += dot(hid[g][origin], wdb[origin], TN)
        pack(lambda c: oacc[g][:, c * LANE : (c + 1) * LANE], g, send2[g])
        exchange(g, send2[g], recv2[g], ret_s.at[g], ret_r.at[g])

    for g, (s0, ns) in enumerate(groups):
        n_rows = ns * n_dp
        exchange_wait(g, recv2[g], ret_r.at[g])

        def keep(q, cols):
            for c, v in enumerate(cols):
                oacc[g][q * n_dp : (q + 1) * n_dp, c * LANE : (c + 1) * LANE] = v

        unpack(recv2[g], g, keep)
        for h in range(2):
            z = oacc[g][:, h * feats : (h + 1) * feats].astype(BF)
            cols = slice(s0 * n_dp, (s0 + ns) * n_dp)
            m = dot(ct[0, :, cols], z) + dot(ct[1, :, cols], z)
            mixs[h] = m if g == 0 else mixs[h] + m
    last = rcopy(mixs.at[other], mixr, mix_s, mix_r, (d, t, other))
    last.start()
    last.wait_recv()
    out[...] = (mixs[s] + mixr[...]).astype(BF)

    last.wait_send()
    for c in pairs:
        c.wait_send()
    wait_bytes(wdb.at[pl.ds(0, n_t - 1)], wd_s)
    wait_bytes(lr.at[pl.ds(0, n_t - 1)], lp_s)
    wait_bytes(lg.at[pl.ds(0, n_t - 1)], lg_s)
    for g, (s0, ns) in enumerate(groups):
        exchange_wait(g, recv[g], dis_s.at[g])
        exchange_wait(g, recv2[g], ret_s.at[g])
        wait_bytes(ss.at[pl.ds(0, n_t - 1), :, pl.ds(s0 * n_dp, ns * n_dp)], ss_s.at[g])
        ref_of = lambda o, h, g=g: ag[g].at[o, h]
        for hop in range(1, hops + 1):
            for h, direction in legs(hop):
                ring(ref_of, ag_s.at[g], ag_r.at[g], 2, hop, direction, h).wait_send()
            for direction in range(2):
                h = None if hop < hops else direction
                ref = hid[g].at[t] if h is None else hid[g].at[t, pl.ds(h * (hid_n // 2), hid_n // 2)]
                pltpu.make_async_copy(ref, ref, hid_s.at[g, direction * hops + hop - 1]).wait()


def body(tokens, gain, router, routes, w_gate, w_up, w_down):
    toks, feats = tokens.shape
    top = routes.shape[1]
    n_dp, n_t, n_side = (lax.axis_size(a) for a in ("dp", "tensor", "side"))
    experts = n_dp * n_side
    slots = min(toks, max(2, toks * top * 5 // (experts * 4)))
    hid_n = w_gate.shape[2]
    groups = split_slots(slots)
    chunks = 2 * feats // LANE
    n_rows = [ns * n_dp for _, ns in groups]
    planes = [n_dp * plane_rows(ns, chunks) for _, ns in groups]
    rows = slots * n_dp
    hops = n_t // 2
    piece = toks // n_t
    cfg = (n_dp, n_t, slots, groups, toks, feats, experts, top, hid_n)
    vm = pltpu.VMEM
    dma = pltpu.SemaphoreType.DMA
    ng = len(groups)
    plane_bufs = [vm((p, LANE), BF) for p in planes]
    scratch = (
        [
            vm((2, toks, feats), BF),
            vm((2, feats, experts), BF),
            vm((2, 8, feats), F32),
            vm((rows, toks), BF),
            vm((max(planes), LANE), F32),
            vm((n_t, 2, piece, experts), F32),
            vm((n_t, 2, piece, experts), F32),
            vm((n_t, piece, experts), F32),
            vm((n_t, 8, rows), F32),
            vm((n_t, 2, 2 * hid_n, feats), BF),
            vm((n_t, hid_n, 2 * feats), BF),
            vm((2, toks, rows), BF),
            vm((2, toks, feats), F32),
            vm((toks, feats), F32),
        ]
        + plane_bufs * 4
        + [vm((n_t, 2, n, feats), BF) for n in n_rows]
        + [vm((n_t, hid_n, n), BF) for n in n_rows]
        + [vm((2 * hid_n, n), F32) for n in n_rows]
        + [vm((n, 2 * feats), F32) for n in n_rows]
        + [dma((3,)), dma((3,))]
        + [dma] * 8
        + [dma((ng,))] * 6
        + [dma((ng, 4 * hops))] * 2
        + [dma((ng, 2 * hops))] * 2
    )
    return pl.pallas_call(
        functools.partial(kernel, cfg),
        out_shape=jax.ShapeDtypeStruct((toks, feats), BF),
        in_specs=[pl.BlockSpec(memory_space=vm)] * 7,
        out_specs=pl.BlockSpec(memory_space=vm),
        scratch_shapes=scratch,
        compiler_params=pltpu.CompilerParams(
            collective_id=0, has_side_effects=True, vmem_limit_bytes=56 * 1024 * 1024
        ),
        name="routed_experts",
    )(tokens, gain.reshape(1, feats), router, routes, w_gate, w_up, w_down)


def solution(mesh):
    placed = (
        P("dp", ("tensor", "side")),
        P(("tensor", "side")),
        P(("tensor", "side"), None),
        P("dp", None),
        P(("dp", "side"), None, "tensor"),
        P(("dp", "side"), None, "tensor"),
        P(("dp", "side"), "tensor", None),
    )
    return jax.shard_map(
        body, mesh=mesh, in_specs=placed, out_specs=P("dp", ("tensor", "side")), check_vma=False
    )
```

time: 410 us -> 158 us (0.39)
  waiting for transfers between devices: 257 us -> 0 us
  Pallas kernels: 0 us -> 150 us
  blocking collectives: 88 us -> 0 us
  matrix products: 17.6 us -> 0 us
  starting transfers between devices: 14 us -> 0 us
  between operations: 13.2 us -> 0.01 us
  other arithmetic: 9.96 us -> 0 us
    pallas_call x0 -> x1, Pallas kernels: none -> 150 us  [body(): pl.pallas_call(functools.partial(kernel, cfg), out_shape=jax.ShapeDtypeSt...]
    psum x1 -> x0, waiting for transfers between devices: 106 us -> none  [body(): lax.psum(jnp.dot(scaled, router_f, precision=lax.Precision.HIGHEST), ('te...]
    reduce_scatter x1 -> x0, waiting for transfers between devices: 70 us -> none  [body(): lax.psum_scatter(lax.dot_general(down_w, hidden, (((0,), (1,)), ((), ()))...]
    all_gather x1 -> x0, waiting for transfers between devices: 64.6 us -> none  [body(): piece = lax.all_gather(rows_in, 'tensor', axis=1, tiled=True)]
    all_to_all x3 -> x0, blocking collectives: 50.9 us -> none  [the longest x1 38.7 us: body(): lax.all_to_all(paired.reshape(n_dp, slots, feats * n_side), 'dp', split_a...]
    psum x1 -> x0, blocking collectives: 37.1 us -> none  [body(): total = lax.psum(square, ('tensor', 'side'))]
    dot_general x5 -> x0, matrix products: 17.6 us -> none  [the longest x1 8.59 us: body(): lax.dot_general(down_w, hidden, (((0,), (1,)), ((), ())), preferred_eleme...]
    all_to_all x1 -> x0, waiting for transfers between devices: 16.3 us -> none  [body(): lax.all_to_all(back, 'dp', split_axis=2, concat_axis=2, tiled=True)]
  transfers between devices with their start and end apart: 4 -> 0, of which waited for: 4 -> 0; matrix products, arithmetic and copies ran while one was open for 2% -> 0% of each run, Pallas kernels for 0% -> 0%
where the time goes in v1:
time: 158 us; the launch traced here: 157 us
  Pallas kernels  150 us (95%)
  local copies, waits for them, and re-layouts  7.73 us (5%)
    pallas_call x1, Pallas kernels, body(): pl.pallas_call(functools.partial(kernel, cfg), out_shape=jax.ShapeDtypeSt...  150 us
    unnamed x6, local copies, waits for them, and re-layouts  6.51 us

profile of v1, /device:TPU:1, one launch (start us, length us, event | category | flops | bytes accessed | tf_op | source)
XLA Modules:
  0.0 157.3 jit_solution(12402717795578971695)
XLA Ops:
  0.0 1.2 reshape.3.refs_1_
  1.2 1.4 copy.8.refs_3_
  2.6 0.0 copy-start
  2.6 2.3 %copy.9.refs_4_ = bf16[1,4096,96]{2,1,0:T(8,128)(2,1)} copy(bf16[1,4096,96]{1,2,0:T(8,128)(2,1)} %param.11) | data formatting | bytes 1572864 | tf_op args[4]
  4.9 0.0 copy-done
  5.0 1.3 copy.10.refs_5_
  6.3 149.5 %routed_experts.1 = bf16[128,256]{1,0:T(8,128)(2,1)} custom-call(bf16[128,256]{1,0:T(8,128)(2,1)} %refs_0_.1, bf16[1,256]{1,0:T(2,128)(2,1)} %reshape.3.refs_1_, bf16[256,128]{1,0:T(8,128)(2,1)} %refs_2_.1, s32[128,8]{1,0:T(8,128)} %copy.8.refs_3_, bf16[1,4096,96]{2,1,0:T(8,128)(2,1)} %copy.9.refs_4_, bf16[1,4096,96]{2,1,0:T(8,128)(2,1)} %copy.10.refs_5_, ...), custom_call_target="tpu_custom_call" | custom-call | tf_op jit(solution)/shard_map/routed_experts/pallas_call | solution.py:413
  155.8 1.5 copy.12
Async XLA Ops:
  2.6 2.3 %copy-start = (bf16[1,4096,96]{1,2,0:T(8,128)(2,1)S(1)}, bf16[1,4096,96]{1,2,0:T(8,128)(2,1)}, u32[]{:S(2)}) copy-start(bf16[1,4096,96]{1,2,0:T(8,128)(2,1)} %param.12) | copy-start | bytes 2359300

commit v2 on v1

v2 whole, which is shorter than its diff:
```python
import functools

import jax
import jax.numpy as jnp
from jax import lax
from jax.experimental import pallas as pl
from jax.experimental.pallas import tpu as pltpu
from jax.sharding import PartitionSpec as P

MESH = pl.DeviceIdType.MESH
BF = jnp.bfloat16
F32 = jnp.float32
LANE = 128
HIGH = lax.Precision.HIGHEST
NT = (((1,), (1,)), ((), ()))
TN = (((0,), (0,)), ((), ()))


def dot(a, b, dims=(((1,), (0,)), ((), ())), precision=None):
    return lax.dot_general(a, b, dims, precision=precision, preferred_element_type=F32)


def split_slots(slots):
    return ((0, slots),)


def plane_rows(count, chunks):
    return -(-count * chunks // 8) * 8


def schedule(ng, gather_hops, unit_hops):
    steps = [("rows", 0)] + [("gather", 0, k) for k in range(1, gather_hops)] + [("far", 0, 0), ("far", 0, 1)]
    steps += [("gather", 0, gather_hops), ("hidden", 0)]
    return steps + [("units", 0, k) for k in range(1, unit_hops + 1)] + [("back", 0)]


def kernel(cfg, *refs):
    n_dp, n_t, slots, groups, toks, feats, experts, top, hid_n = cfg
    it = iter(refs)
    take = lambda n: [next(it) for _ in range(n)]
    tokens, gain, router, routes, w_gate, w_up, w_down, out = take(8)
    xtok, xg, far, rt, gn, chosen, tmp, lp, lr, lg, ss, wt, wdb, ct, mixs, mixr = take(16)
    ng = len(groups)
    send, recv = take(3 * ng), take(3 * ng)
    send2, recv2, ag, hid, acc, oacc = [take(ng) for _ in range(6)]
    pair_s, pair_r, far_s, far_r, wd_s, wd_r, lp_s, lp_r, lg_s, lg_r, mix_s, mix_r, wt_r, wl_r = take(14)
    dis_s, dis_r, ret_s, ret_r, ss_s, ss_r, ag_s, ag_r, hid_s, hid_r = take(10)

    d, t, s = lax.axis_index("dp"), lax.axis_index("tensor"), lax.axis_index("side")
    nz = 8 if n_dp % 8 == 0 else n_dp
    nx = n_dp // nz
    chunks = 2 * feats // LANE
    per_half = feats // LANE
    piece = toks // n_t
    width = 2 * feats * n_t
    rows = slots * n_dp
    other = 1 - s
    gather_hops, unit_hops = n_t // 2 - 1, n_t // 2
    left_over = []

    def dp_peer(i):
        return lax.rem(d // nz + i // nz, nx) * nz + lax.rem(d % nz + i % nz, nz)

    def t_peer(i):
        return lax.rem(t + i, n_t)

    def rcopy(src, dst, ssem, rsem, dev):
        return pltpu.make_async_remote_copy(
            src_ref=src, dst_ref=dst, send_sem=ssem, recv_sem=rsem, device_id=dev, device_id_type=MESH
        )

    def wait_bytes(ref, sem):
        pltpu.make_async_copy(ref, ref, sem).wait()

    def later(f, *args):
        left_over.append(lambda: f(*args))

    barrier = pltpu.get_barrier_semaphore()
    pl.semaphore_signal(barrier, inc=1, device_id=(d, t, other), device_id_type=MESH)

    def greet_t(i, carry):
        pl.semaphore_signal(barrier, inc=1, device_id=(d, t_peer(i), s), device_id_type=MESH)
        return carry

    def greet_dp(i, carry):
        pl.semaphore_signal(barrier, inc=1, device_id=(dp_peer(i), t, s), device_id_type=MESH)
        return carry

    lax.fori_loop(1, n_t, greet_t, 0)
    lax.fori_loop(1, n_dp, greet_dp, 0)

    def weights_in(j, carry):
        for h in range(2):
            k0 = pl.ds(pl.multiple_of(j * 2 * feats + h * feats, feats), feats)
            pltpu.make_async_copy(w_gate.at[0, :, k0], wt.at[j, h, pl.ds(0, hid_n)], wt_r).start()
            pltpu.make_async_copy(w_up.at[0, :, k0], wt.at[j, h, pl.ds(hid_n, hid_n)], wt_r).start()
        return carry

    lax.fori_loop(0, n_t, weights_in, 0)
    down_cols = lambda p: pl.ds(pl.multiple_of(p * 2 * feats, 2 * feats), 2 * feats)
    own_down = pltpu.make_async_copy(w_down.at[0, :, down_cols(t)], wdb.at[t], wl_r)
    own_down.start()

    e_ids = lax.broadcasted_iota(jnp.int32, (experts, toks), 0)
    routes_v = routes[...]
    onehot = jnp.zeros((experts, toks), F32)
    for k in range(top):
        onehot = onehot + jnp.where(routes_v[k : k + 1, :] == e_ids, 1.0, 0.0)
    earlier = jnp.where(
        lax.broadcasted_iota(jnp.int32, (toks, toks), 0) < lax.broadcasted_iota(jnp.int32, (toks, toks), 1), 1.0, 0.0
    )
    before = dot(onehot.astype(BF), earlier.astype(BF))
    taken = (onehot * (before + 1.0)).astype(BF)

    r_of = lax.broadcasted_iota(jnp.int32, (rows, experts), 0)
    expand = jnp.where(
        lax.broadcasted_iota(jnp.int32, (rows, experts), 1) == 2 * (r_of % n_dp) + s, 1.0, 0.0
    ).astype(BF)
    slot_of = lax.broadcasted_iota(jnp.int32, (rows, toks), 0) // n_dp + 1
    chosen[...] = jnp.where(dot(expand, taken) == slot_of.astype(F32), 1.0, 0.0).astype(BF)
    gn[s] = jnp.broadcast_to(gain[...].astype(F32), (8, feats))
    xtok[s] = tokens[...]
    xg[...] = (tokens[...].astype(F32) * gn[s, 0:1]).astype(BF)
    rt[s] = router[...]
    tmp[...] = jnp.zeros_like(tmp)

    pl.semaphore_wait(barrier, 1 + (n_t - 1) + (n_dp - 1))

    pairs = [
        rcopy(ref, ref, pair_s.at[i], pair_r.at[i], (d, t, other))
        for i, ref in enumerate((xtok.at[s], rt.at[s], gn.at[s]))
    ]
    for c in pairs:
        c.start()
        later(c.wait_send)

    last_hop = gather_hops
    far_targets = [t_peer(n_t // 2), t_peer((n_t - last_hop) + s * (2 * last_hop - n_t))]
    fars = [
        rcopy(xg, far.at[j, s], far_s.at[j], far_r.at[j], (d, p, s)) for j, p in enumerate(far_targets)
    ]
    for c in fars:
        c.start()
        later(c.wait_send)

    def wd_send(i, carry):
        p = t_peer(i)
        rcopy(w_down.at[0, :, down_cols(p)], wdb.at[t], wd_s, wd_r, (d, p, s)).start()
        return carry

    lax.fori_loop(1, n_t, wd_send, 0)
    later(wait_bytes, wdb.at[pl.ds(0, n_t - 1)], wd_s)

    def pack(value_of, g, dst):
        s0, ns = groups[g]
        pr = plane_rows(ns, chunks)
        for c in range(chunks):
            v = value_of(c)
            for q in range(ns):
                tmp[pl.ds(c * ns + q, n_dp, stride=pr), :] = v[q * n_dp : (q + 1) * n_dp]
        dst[...] = tmp[: n_dp * pr].astype(BF).reshape(n_dp, pr, LANE)

    def exchange(src, dst, ssem, rsem):
        def one(i, carry):
            p = dp_peer(i)
            rcopy(src.at[p], dst.at[d], ssem, rsem, (p, t, s)).start()
            return carry

        lax.fori_loop(1, n_dp, one, 0)
        dst[d] = src[d]
        later(exchange_wait, src, ssem)

    def exchange_wait(dst, sem):
        wait_bytes(dst.at[pl.ds(0, n_dp - 1)], sem)

    def dispatch(j, sources):
        for g, (s0, ns) in enumerate(groups):
            sel = chosen[s0 * n_dp : (s0 + ns) * n_dp]
            halves = [dot(sel, src) for src in sources]
            k = j * ng + g
            pack(lambda c: halves[c // per_half][:, (c % per_half) * LANE : (c % per_half + 1) * LANE], g, send[k])
            exchange(send[k], recv[k], dis_s.at[k], dis_r.at[k])

    pairs[0].wait_recv()
    dispatch(0, [xtok[h] for h in range(2)])
    swaps = [rcopy(far.at[j, s], far.at[j, s], far_s.at[2 + j], far_r.at[2 + j], (d, t, other)) for j in range(2)]
    for j in range(2):
        fars[j].wait_recv()
        swaps[j].start()
        later(swaps[j].wait_send)
    for j in range(2):
        swaps[j].wait_recv()
        dispatch(1 + j, [far[j, h] for h in range(2)])

    for c in pairs[1:]:
        c.wait_recv()
    part = jnp.zeros((toks, experts), F32)
    sq = jnp.zeros((toks, 1), F32)
    for h in range(2):
        xf = xtok[h].astype(F32)
        sq = sq + jnp.sum(xf * xf, axis=1, keepdims=True)
        part = part + dot(xf * gn[h][0:1], rt[h].astype(F32), precision=HIGH)
    for j in range(n_t):
        lp[j, 0] = part[j * piece : (j + 1) * piece]
        lp[j, 1] = jnp.broadcast_to(sq[j * piece : (j + 1) * piece], (piece, experts))

    def lp_send(i, carry):
        p = t_peer(i)
        rcopy(lp.at[p], lr.at[t], lp_s, lp_r, (d, p, s)).start()
        return carry

    lax.fori_loop(1, n_t, lp_send, 0)
    later(wait_bytes, lr.at[pl.ds(0, n_t - 1)], lp_s)
    lr[t] = lp[t]
    wait_bytes(lr.at[pl.ds(0, n_t - 1)], lp_r)
    tot = lr[0]
    for j in range(1, n_t):
        tot = tot + lr[j]
    lg[t] = tot[0] * lax.rsqrt(tot[1] / width + 1e-06)

    def lg_send(i, carry):
        rcopy(lg.at[t], lg.at[t], lg_s, lg_r, (d, t_peer(i), s)).start()
        return carry

    lax.fori_loop(1, n_t, lg_send, 0)
    later(wait_bytes, lg.at[pl.ds(0, n_t - 1)], lg_s)

    r_of = lax.broadcasted_iota(jnp.int32, (experts, rows), 1)
    expand_t = jnp.where(
        lax.broadcasted_iota(jnp.int32, (experts, rows), 0) == 2 * (r_of % n_dp) + s, 1.0, 0.0
    ).astype(BF)
    slot_of = lax.broadcasted_iota(jnp.int32, (toks, rows), 1) // n_dp + 1
    mine = dot(taken, expand_t, TN) == slot_of.astype(F32)
    wait_bytes(lg.at[pl.ds(0, n_t - 1)], lg_r)
    logits = jnp.concatenate([lg[j] for j in range(n_t)], axis=0).T
    masked = jnp.where(onehot > 0.0, logits, -jnp.inf)
    ex = jnp.exp(masked - jnp.max(masked, axis=0, keepdims=True))
    weights = ex / jnp.sum(ex, axis=0, keepdims=True)
    w_hi = weights.astype(BF)
    w_lo = (weights - w_hi.astype(F32)).astype(BF)
    ct[0] = jnp.where(mine, dot(w_hi, expand_t, TN), 0.0).astype(BF)
    ct[1] = jnp.where(mine, dot(w_lo, expand_t, TN), 0.0).astype(BF)
    wait_bytes(wt, wt_r)
    own_down.wait()

    right, left = t_peer(1), t_peer(n_t - 1)
    hops = gather_hops

    def ring(g, hop, direction, h, incoming):
        step = hop if incoming else hop - 1
        origin = t_peer((n_t - step) % n_t) if direction == 0 else t_peer(step)
        ref = ag[g].at[origin, h]
        k = (direction * hops + hop - 1) * 2 + h
        return origin, rcopy(
            ref, ref, ag_s.at[g, k], ag_r.at[g, k], (d, right if direction == 0 else left, s)
        )

    def ring_start(g, hop, direction, h):
        c = ring(g, hop, direction, h, False)[1]
        c.start()
        later(c.wait_send)

    def legs(hop):
        if hop < hops:
            return [(h, direction) for h in range(2) for direction in range(2)]
        return [(0, 0), (1, 1)]

    def unpack(src, g, use):
        s0, ns = groups[g]
        pr = plane_rows(ns, chunks)
        tmp[: n_dp * pr] = src[...].astype(F32).reshape(n_dp * pr, LANE)
        for q in range(ns):
            use(q, [tmp[pl.ds(c * ns + q, n_dp, stride=pr), :] for c in range(chunks)])

    def do_rows(g):
        s0, ns = groups[g]
        exchange_wait(recv[g], dis_r.at[g])
        squares = []

        def scale(q, cols):
            squares.append(sum(v * v for v in cols))
            for c, v in enumerate(cols):
                h, l0 = c // per_half, (c % per_half) * LANE
                ag[g][t, h, q * n_dp : (q + 1) * n_dp, l0 : l0 + LANE] = (v * gn[h][0:1, l0 : l0 + LANE]).astype(BF)

        unpack(recv[g], g, scale)
        for h, direction in legs(1):
            ring_start(g, 1, direction, h)
        ones = jnp.ones((8, LANE), F32)
        cols = pl.ds(s0 * n_dp, ns * n_dp)
        for q in range(ns):
            ss[t, :, (s0 + q) * n_dp : (s0 + q + 1) * n_dp] = dot(ones, squares[q], NT, precision=HIGH)

        def ss_send(i, carry):
            rcopy(ss.at[t, :, cols], ss.at[t, :, cols], ss_s.at[g], ss_r.at[g], (d, t_peer(i), s)).start()
            return carry

        lax.fori_loop(1, n_t, ss_send, 0)
        later(wait_bytes, ss.at[pl.ds(0, n_t - 1), :, cols], ss_s.at[g])
        acc[g][...] = dot(wt[t, 0], ag[g][t, 0], NT) + dot(wt[t, 1], ag[g][t, 1], NT)

    def do_far(g, j):
        k = (1 + j) * ng + g
        exchange_wait(recv[k], dis_r.at[k])
        origins = [t_peer(n_t // 2)] * 2 if j == 0 else [t_peer(last_hop), t_peer(n_t - last_hop)]

        def keep(q, cols):
            for c, v in enumerate(cols):
                h, l0 = c // per_half, (c % per_half) * LANE
                ag[g][origins[h], h, q * n_dp : (q + 1) * n_dp, l0 : l0 + LANE] = v.astype(BF)

        unpack(recv[k], g, keep)
        for h, o in enumerate(origins):
            acc[g][...] += dot(wt[o, h], ag[g][o, h], NT)

    def do_gather(g, hop):
        going = legs(hop + 1) if hop < hops else []
        for h, direction in legs(hop):
            origin, c = ring(g, hop, direction, h, True)
            c.wait_recv()
            if (h, direction) in going:
                ring_start(g, hop + 1, direction, h)
            acc[g][...] += dot(wt[origin, h], ag[g][origin, h], NT)

    half = hid_n // 2

    def unit_legs(hop):
        if hop < unit_hops:
            return [(h, direction) for h in range(2) for direction in range(2)]
        return [(0, 0), (1, 1)]

    def units(g, hop, direction, h, incoming):
        step = hop if incoming else hop - 1
        origin = t_peer((n_t - step) % n_t) if direction == 0 else t_peer(step)
        ref = hid[g].at[origin, pl.ds(h * half, half)]
        k = (direction * unit_hops + hop - 1) * 2 + h
        return origin, rcopy(
            ref, ref, hid_s.at[g, k], hid_r.at[g, k], (d, right if direction == 0 else left, s)
        )

    def units_start(g, hop, direction, h):
        c = units(g, hop, direction, h, False)[1]
        c.start()
        later(c.wait_send)

    def do_hidden(g):
        s0, ns = groups[g]
        cols = slice(s0 * n_dp, (s0 + ns) * n_dp)
        wait_bytes(ss.at[pl.ds(0, n_t - 1), :, pl.ds(s0 * n_dp, ns * n_dp)], ss_r.at[g])
        total = ss[0, 0:1, cols]
        for j in range(1, n_t):
            total = total + ss[j, 0:1, cols]
        rinv = lax.rsqrt(total / width + 1e-06)
        gate = acc[g][0:hid_n] * rinv
        hid[g][t] = (gate * jax.nn.sigmoid(gate) * (acc[g][hid_n : 2 * hid_n] * rinv)).astype(BF)
        for h, direction in unit_legs(1):
            units_start(g, 1, direction, h)
        if g == 0:
            wait_bytes(wdb.at[pl.ds(0, n_t - 1)], wd_r)
        oacc[g][...] = dot(hid[g][t], wdb[t], TN)

    def do_units(g, hop):
        got = [None, None]
        going = unit_legs(hop + 1) if hop < unit_hops else []
        for h, direction in unit_legs(hop):
            origin, c = units(g, hop, direction, h, True)
            c.wait_recv()
            got[direction] = origin
            if (h, direction) in going:
                units_start(g, hop + 1, direction, h)
        for origin in got if hop < unit_hops else got[:1]:
            oacc[g][...] += dot(hid[g][origin], wdb[origin], TN)

    def do_back(g):
        pack(lambda c: oacc[g][:, c * LANE : (c + 1) * LANE], g, send2[g])
        exchange(send2[g], recv2[g], ret_s.at[g], ret_r.at[g])

    does = {"rows": do_rows, "far": do_far, "gather": do_gather, "hidden": do_hidden, "units": do_units, "back": do_back}
    for name, *args in schedule(ng, gather_hops, unit_hops):
        does[name](*args)

    for g, (s0, ns) in enumerate(groups):
        exchange_wait(recv2[g], ret_r.at[g])

        def keep(q, cols):
            for c, v in enumerate(cols):
                oacc[g][q * n_dp : (q + 1) * n_dp, c * LANE : (c + 1) * LANE] = v

        unpack(recv2[g], g, keep)
        for h in range(2):
            z = oacc[g][:, h * feats : (h + 1) * feats].astype(BF)
            cols = slice(s0 * n_dp, (s0 + ns) * n_dp)
            m = dot(ct[0, :, cols], z) + dot(ct[1, :, cols], z)
            mixs[h] = m if g == 0 else mixs[h] + m
    last = rcopy(mixs.at[other], mixr, mix_s, mix_r, (d, t, other))
    last.start()
    last.wait_recv()
    out[...] = (mixs[s] + mixr[...]).astype(BF)
    later(last.wait_send)

    for f in left_over:
        f()


def body(tokens, gain, router, routes, w_gate, w_up, w_down):
    toks, feats = tokens.shape
    top = routes.shape[1]
    n_dp, n_t, n_side = (lax.axis_size(a) for a in ("dp", "tensor", "side"))
    experts = n_dp * n_side
    slots = min(toks, max(2, toks * top * 5 // (experts * 4)))
    hid_n = w_gate.shape[2]
    groups = split_slots(slots)
    chunks = 2 * feats // LANE
    n_rows = [ns * n_dp for _, ns in groups]
    planes = [plane_rows(ns, chunks) for _, ns in groups]
    rows = slots * n_dp
    gather_hops, unit_hops = n_t // 2 - 1, n_t // 2
    piece = toks // n_t
    cfg = (n_dp, n_t, slots, groups, toks, feats, experts, top, hid_n)
    vm = pltpu.VMEM
    dma = pltpu.SemaphoreType.DMA
    ng = len(groups)
    plane_bufs = [vm((n_dp, p, LANE), BF) for p in planes]
    scratch = (
        [
            vm((2, toks, feats), BF),
            vm((toks, feats), BF),
            vm((2, 2, toks, feats), BF),
            vm((2, feats, experts), BF),
            vm((2, 8, feats), F32),
            vm((rows, toks), BF),
            vm((n_dp * max(planes), LANE), F32),
            vm((n_t, 2, piece, experts), F32),
            vm((n_t, 2, piece, experts), F32),
            vm((n_t, piece, experts), F32),
            vm((n_t, 8, rows), F32),
            vm((n_t, 2, 2 * hid_n, feats), BF),
            vm((n_t, hid_n, 2 * feats), BF),
            vm((2, toks, rows), BF),
            vm((2, toks, feats), F32),
            vm((toks, feats), F32),
        ]
        + plane_bufs * 8
        + [vm((n_t, 2, n, feats), BF) for n in n_rows]
        + [vm((n_t, hid_n, n), BF) for n in n_rows]
        + [vm((2 * hid_n, n), F32) for n in n_rows]
        + [vm((n, 2 * feats), F32) for n in n_rows]
        + [dma((3,)), dma((3,)), dma((4,)), dma((4,))]
        + [dma] * 10
        + [dma((3 * ng,))] * 2
        + [dma((ng,))] * 4
        + [dma((ng, 4 * gather_hops))] * 2
        + [dma((ng, 4 * unit_hops))] * 2
    )
    in_vmem, in_hbm = pl.BlockSpec(memory_space=vm), pl.BlockSpec(memory_space=pl.ANY)
    return pl.pallas_call(
        functools.partial(kernel, cfg),
        out_shape=jax.ShapeDtypeStruct((toks, feats), BF),
        in_specs=[in_vmem] * 4 + [in_hbm] * 3,
        out_specs=in_vmem,
        scratch_shapes=scratch,
        compiler_params=pltpu.CompilerParams(
            collective_id=0, has_side_effects=True, vmem_limit_bytes=56 * 1024 * 1024
        ),
        name="routed_experts",
    )(
        tokens,
        gain,
        router,
        routes.T,
        jnp.swapaxes(w_gate, 1, 2),
        jnp.swapaxes(w_up, 1, 2),
        w_down,
    )


def solution(mesh):
    placed = (
        P("dp", ("tensor", "side")),
        P(("tensor", "side")),
        P(("tensor", "side"), None),
        P("dp", None),
        P(("dp", "side"), None, "tensor"),
        P(("dp", "side"), None, "tensor"),
        P(("dp", "side"), "tensor", None),
    )
    return jax.shard_map(
        body, mesh=mesh, in_specs=placed, out_specs=P("dp", ("tensor", "side")), check_vma=False
    )
```

time: 158 us -> 139 us (0.88)
  Pallas kernels: 150 us -> 137 us
  local copies, waits for them, and re-layouts: 7.73 us -> 1.47 us
    pallas_call x1, Pallas kernels: 150 us -> 137 us  [body(): pl.pallas_call(functools.partial(kernel, cfg), out_shape=jax.ShapeDtypeSt...]
    unnamed x6 -> x1, local copies, waits for them, and re-layouts: 6.51 us -> 1.47 us
where the time goes in v2:
time: 139 us
  Pallas kernels  137 us (99%)
  local copies, waits for them, and re-layouts  1.47 us (1%)
    pallas_call x1, Pallas kernels, body(): pl.pallas_call(functools.partial(kernel, cfg), out_shape=jax.ShapeDtypeSt...  137 us

profile of v2, /device:TPU:1, one launch (start us, length us, event | category | flops | bytes accessed | tf_op | source)
XLA Modules:
  0.0 138.7 jit_solution(12621677544537754557)
XLA Ops:
  0.0 137.3 %routed_experts.1 = bf16[128,256]{1,0:T(8,128)(2,1)} custom-call(bf16[128,256]{1,0:T(8,128)(2,1)} %refs_0_.1, bf16[256]{0:T(256)(128)(2,1)} %refs_1_.1, bf16[256,128]{1,0:T(8,128)(2,1)} %refs_2_.1, s32[8,128]{1,0:T(8,128)} %bitcast.5, bf16[1,96,4096]{2,1,0:T(8,128)(2,1)} %bitcast.3, bf16[1,96,4096]{2,1,0:T(8,128)(2,1)} %bitcast.4, bf16[1,96,4096]{2,1,0:T(8,128)(2,1)} %refs_6_.1), custom_call_target="tpu_custom_call" | custom-call | tf_op jit(solution)/shard_map/routed_experts/pallas_call | solution.py:456
  137.3 1.5 %copy.9 = bf16[128,256]{1,0:T(8,128)(2,1)} copy(bf16[128,256]{1,0:T(8,128)(2,1)} %routed_experts.1) | data formatting | bytes 131072

commit v3 on v2

--- a/solution.py
+++ b/solution.py
@@ -21,7 +21,7 @@
 
 
 def split_slots(slots):
-    return ((0, slots),)
+    return ((0, slots - 2), (slots - 2, 2))
 
 
 def plane_rows(count, chunks):
@@ -29,9 +29,16 @@
 
 
 def schedule(ng, gather_hops, unit_hops):
-    steps = [("rows", 0)] + [("gather", 0, k) for k in range(1, gather_hops)] + [("far", 0, 0), ("far", 0, 1)]
-    steps += [("gather", 0, gather_hops), ("hidden", 0)]
-    return steps + [("units", 0, k) for k in range(1, unit_hops + 1)] + [("back", 0)]
+    steps = [("farsend", 0), ("rows",), ("farsend", 1), ("logits",)]
+    for k in range(1, gather_hops):
+        steps += [("gather", g, k) for g in range(ng)]
+    steps += [("weights",), ("far", 0), ("far", 1)]
+    for g in range(ng):
+        steps += [("gather", g, gather_hops), ("hidden", g)]
+    for k in range(1, unit_hops + 1):
+        for g in range(ng):
+            steps += [("units", g, k)] + ([("back", g)] if k == unit_hops else [])
+    return steps
 
 
 def kernel(cfg, *refs):
@@ -39,10 +46,10 @@
     it = iter(refs)
     take = lambda n: [next(it) for _ in range(n)]
     tokens, gain, router, routes, w_gate, w_up, w_down, out = take(8)
-    xtok, xg, far, rt, gn, chosen, tmp, lp, lr, lg, ss, wt, wdb, ct, mixs, mixr = take(16)
+    xtok, xg, far, stage_x, stage_w, rt, gn, chosen, tmp, lp, lr, lg, ss, wt, wdb, ct, mixs, mixr = take(18)
     ng = len(groups)
-    send, recv = take(3 * ng), take(3 * ng)
-    send2, recv2, ag, hid, acc, oacc = [take(ng) for _ in range(6)]
+    send, recv = take(3), take(3)
+    send2, recv2, hid, oacc, ag, acc = [take(ng) for _ in range(6)]
     pair_s, pair_r, far_s, far_r, wd_s, wd_r, lp_s, lp_r, lg_s, lg_r, mix_s, mix_r, wt_r, wl_r = take(14)
     dis_s, dis_r, ret_s, ret_r, ss_s, ss_r, ag_s, ag_r, hid_s, hid_r = take(10)
 
@@ -101,6 +108,42 @@
     own_down = pltpu.make_async_copy(w_down.at[0, :, down_cols(t)], wdb.at[t], wl_r)
     own_down.start()
 
+    gn[s] = jnp.broadcast_to(gain[...].astype(F32), (8, feats))
+    xtok[s] = tokens[...]
+    xg[...] = (tokens[...].astype(F32) * gn[s, 0:1]).astype(BF)
+    rt[s] = router[...]
+    tmp[...] = jnp.zeros_like(tmp)
+
+    pl.semaphore_wait(barrier, 1 + (n_t - 1) + (n_dp - 1))
+
+    pairs = [
+        rcopy(ref, ref, pair_s.at[i], pair_r.at[i], (d, t, other))
+        for i, ref in enumerate((xtok.at[s], rt.at[s], gn.at[s]))
+    ]
+    for c in pairs:
+        c.start()
+        later(c.wait_send)
+
+    half_way = n_t // 2
+    near = (d, t_peer(1 + s * (n_t - 2)), s)
+    onward = (d, t_peer(gather_hops + s * (n_t - 2 * gather_hops)), s)
+    staged_x = rcopy(xg, stage_x, far_s.at[0], far_r.at[0], near)
+    staged_w = rcopy(w_down.at[0, :, down_cols(t_peer(half_way))], stage_w, far_s.at[1], far_r.at[1], near)
+    b_peer = t_peer((n_t - gather_hops) + s * (2 * gather_hops - n_t))
+    far_b = rcopy(xg, far.at[1, s], far_s.at[2], far_r.at[2], (d, b_peer, s))
+    for c in (staged_x, far_b, staged_w):
+        c.start()
+        later(c.wait_send)
+
+    def wd_send(i, carry):
+        p = t_peer(i)
+        rcopy(w_down.at[0, :, down_cols(p)], wdb.at[t], wd_s, wd_r, (d, p, s)).start()
+        return carry
+
+    lax.fori_loop(1, half_way, wd_send, 0)
+    lax.fori_loop(half_way + 1, n_t, wd_send, 0)
+    later(wait_bytes, wdb.at[pl.ds(0, n_t - 2)], wd_s)
+
     e_ids = lax.broadcasted_iota(jnp.int32, (experts, toks), 0)
     routes_v = routes[...]
     onehot = jnp.zeros((experts, toks), F32)
@@ -118,41 +161,7 @@
     ).astype(BF)
     slot_of = lax.broadcasted_iota(jnp.int32, (rows, toks), 0) // n_dp + 1
     chosen[...] = jnp.where(dot(expand, taken) == slot_of.astype(F32), 1.0, 0.0).astype(BF)
-    gn[s] = jnp.broadcast_to(gain[...].astype(F32), (8, feats))
-    xtok[s] = tokens[...]
-    xg[...] = (tokens[...].astype(F32) * gn[s, 0:1]).astype(BF)
-    rt[s] = router[...]
-    tmp[...] = jnp.zeros_like(tmp)
-
-    pl.semaphore_wait(barrier, 1 + (n_t - 1) + (n_dp - 1))
-
-    pairs = [
-        rcopy(ref, ref, pair_s.at[i], pair_r.at[i], (d, t, other))
-        for i, ref in enumerate((xtok.at[s], rt.at[s], gn.at[s]))
-    ]
-    for c in pairs:
-        c.start()
-        later(c.wait_send)
-
-    last_hop = gather_hops
-    far_targets = [t_peer(n_t // 2), t_peer((n_t - last_hop) + s * (2 * last_hop - n_t))]
-    fars = [
-        rcopy(xg, far.at[j, s], far_s.at[j], far_r.at[j], (d, p, s)) for j, p in enumerate(far_targets)
-    ]
-    for c in fars:
-        c.start()
-        later(c.wait_send)
-
-    def wd_send(i, carry):
-        p = t_peer(i)
-        rcopy(w_down.at[0, :, down_cols(p)], wdb.at[t], wd_s, wd_r, (d, p, s)).start()
-        return carry
-
-    lax.fori_loop(1, n_t, wd_send, 0)
-    later(wait_bytes, wdb.at[pl.ds(0, n_t - 1)], wd_s)
-
-    def pack(value_of, g, dst):
-        s0, ns = groups[g]
+    def pack(value_of, ns, dst):
         pr = plane_rows(ns, chunks)
         for c in range(chunks):
             v = value_of(c)
@@ -174,23 +183,29 @@
         wait_bytes(dst.at[pl.ds(0, n_dp - 1)], sem)
 
     def dispatch(j, sources):
-        for g, (s0, ns) in enumerate(groups):
-            sel = chosen[s0 * n_dp : (s0 + ns) * n_dp]
-            halves = [dot(sel, src) for src in sources]
-            k = j * ng + g
-            pack(lambda c: halves[c // per_half][:, (c % per_half) * LANE : (c % per_half + 1) * LANE], g, send[k])
-            exchange(send[k], recv[k], dis_s.at[k], dis_r.at[k])
+        halves = [dot(chosen[...], src) for src in sources]
+        pack(
+            lambda c: halves[c // per_half][:, (c % per_half) * LANE : (c % per_half + 1) * LANE], slots, send[j]
+        )
+        exchange(send[j], recv[j], dis_s.at[j], dis_r.at[j])
 
     pairs[0].wait_recv()
     dispatch(0, [xtok[h] for h in range(2)])
-    swaps = [rcopy(far.at[j, s], far.at[j, s], far_s.at[2 + j], far_r.at[2 + j], (d, t, other)) for j in range(2)]
-    for j in range(2):
-        fars[j].wait_recv()
+
+    staged_x.wait_recv()
+    far_a = rcopy(stage_x, far.at[0, s], far_s.at[3], far_r.at[3], onward)
+    far_a.start()
+    later(far_a.wait_send)
+    staged_w.wait_recv()
+    origin_w = t_peer((n_t - 1) - s * (n_t - 2))
+    pass_w = rcopy(stage_w, wdb.at[origin_w], far_s.at[4], wd_r, onward)
+    pass_w.start()
+    later(pass_w.wait_send)
+    swaps = [rcopy(far.at[j, s], far.at[j, s], far_s.at[5 + j], far_r.at[5 + j], (d, t, other)) for j in range(2)]
+    for j, c in ((1, far_b), (0, far_a)):
+        c.wait_recv()
         swaps[j].start()
         later(swaps[j].wait_send)
-    for j in range(2):
-        swaps[j].wait_recv()
-        dispatch(1 + j, [far[j, h] for h in range(2)])
 
     for c in pairs[1:]:
         c.wait_recv()
@@ -212,34 +227,6 @@
     lax.fori_loop(1, n_t, lp_send, 0)
     later(wait_bytes, lr.at[pl.ds(0, n_t - 1)], lp_s)
     lr[t] = lp[t]
-    wait_bytes(lr.at[pl.ds(0, n_t - 1)], lp_r)
-    tot = lr[0]
-    for j in range(1, n_t):
-        tot = tot + lr[j]
-    lg[t] = tot[0] * lax.rsqrt(tot[1] / width + 1e-06)
-
-    def lg_send(i, carry):
-        rcopy(lg.at[t], lg.at[t], lg_s, lg_r, (d, t_peer(i), s)).start()
-        return carry
-
-    lax.fori_loop(1, n_t, lg_send, 0)
-    later(wait_bytes, lg.at[pl.ds(0, n_t - 1)], lg_s)
-
-    r_of = lax.broadcasted_iota(jnp.int32, (experts, rows), 1)
-    expand_t = jnp.where(
-        lax.broadcasted_iota(jnp.int32, (experts, rows), 0) == 2 * (r_of % n_dp) + s, 1.0, 0.0
-    ).astype(BF)
-    slot_of = lax.broadcasted_iota(jnp.int32, (toks, rows), 1) // n_dp + 1
-    mine = dot(taken, expand_t, TN) == slot_of.astype(F32)
-    wait_bytes(lg.at[pl.ds(0, n_t - 1)], lg_r)
-    logits = jnp.concatenate([lg[j] for j in range(n_t)], axis=0).T
-    masked = jnp.where(onehot > 0.0, logits, -jnp.inf)
-    ex = jnp.exp(masked - jnp.max(masked, axis=0, keepdims=True))
-    weights = ex / jnp.sum(ex, axis=0, keepdims=True)
-    w_hi = weights.astype(BF)
-    w_lo = (weights - w_hi.astype(F32)).astype(BF)
-    ct[0] = jnp.where(mine, dot(w_hi, expand_t, TN), 0.0).astype(BF)
-    ct[1] = jnp.where(mine, dot(w_lo, expand_t, TN), 0.0).astype(BF)
     wait_bytes(wt, wt_r)
     own_down.wait()
 
@@ -265,53 +252,63 @@
             return [(h, direction) for h in range(2) for direction in range(2)]
         return [(0, 0), (1, 1)]
 
-    def unpack(src, g, use):
-        s0, ns = groups[g]
+    def unpack(src, ns, use):
         pr = plane_rows(ns, chunks)
         tmp[: n_dp * pr] = src[...].astype(F32).reshape(n_dp * pr, LANE)
         for q in range(ns):
             use(q, [tmp[pl.ds(c * ns + q, n_dp, stride=pr), :] for c in range(chunks)])
 
-    def do_rows(g):
-        s0, ns = groups[g]
-        exchange_wait(recv[g], dis_r.at[g])
+    def group_of(q):
+        for g, (s0, ns) in enumerate(groups):
+            if s0 <= q < s0 + ns:
+                return g, slice((q - s0) * n_dp, (q - s0 + 1) * n_dp)
+
+    def do_rows():
+        exchange_wait(recv[0], dis_r.at[0])
         squares = []
 
         def scale(q, cols):
             squares.append(sum(v * v for v in cols))
+            g, at = group_of(q)
             for c, v in enumerate(cols):
                 h, l0 = c // per_half, (c % per_half) * LANE
-                ag[g][t, h, q * n_dp : (q + 1) * n_dp, l0 : l0 + LANE] = (v * gn[h][0:1, l0 : l0 + LANE]).astype(BF)
-
-        unpack(recv[g], g, scale)
-        for h, direction in legs(1):
-            ring_start(g, 1, direction, h)
+                ag[g][t, h, at, l0 : l0 + LANE] = (v * gn[h][0:1, l0 : l0 + LANE]).astype(BF)
+
+        unpack(recv[0], slots, scale)
+        for g in range(ng):
+            for h, direction in legs(1):
+                ring_start(g, 1, direction, h)
         ones = jnp.ones((8, LANE), F32)
-        cols = pl.ds(s0 * n_dp, ns * n_dp)
-        for q in range(ns):
-            ss[t, :, (s0 + q) * n_dp : (s0 + q + 1) * n_dp] = dot(ones, squares[q], NT, precision=HIGH)
+        for q in range(slots):
+            ss[t, :, q * n_dp : (q + 1) * n_dp] = dot(ones, squares[q], NT, precision=HIGH)
 
         def ss_send(i, carry):
-            rcopy(ss.at[t, :, cols], ss.at[t, :, cols], ss_s.at[g], ss_r.at[g], (d, t_peer(i), s)).start()
+            rcopy(ss.at[t], ss.at[t], ss_s, ss_r, (d, t_peer(i), s)).start()
             return carry
 
         lax.fori_loop(1, n_t, ss_send, 0)
-        later(wait_bytes, ss.at[pl.ds(0, n_t - 1), :, cols], ss_s.at[g])
-        acc[g][...] = dot(wt[t, 0], ag[g][t, 0], NT) + dot(wt[t, 1], ag[g][t, 1], NT)
-
-    def do_far(g, j):
-        k = (1 + j) * ng + g
-        exchange_wait(recv[k], dis_r.at[k])
-        origins = [t_peer(n_t // 2)] * 2 if j == 0 else [t_peer(last_hop), t_peer(n_t - last_hop)]
+        later(wait_bytes, ss.at[pl.ds(0, n_t - 1)], ss_s)
+        for g in range(ng):
+            acc[g][...] = dot(wt[t, 0], ag[g][t, 0], NT) + dot(wt[t, 1], ag[g][t, 1], NT)
+
+    def do_farsend(j):
+        swaps[j].wait_recv()
+        dispatch(1 + j, [far[j, h] for h in range(2)])
+
+    def do_far(j):
+        exchange_wait(recv[1 + j], dis_r.at[1 + j])
+        origins = [t_peer(half_way)] * 2 if j == 0 else [t_peer(gather_hops), t_peer(n_t - gather_hops)]
 
         def keep(q, cols):
+            g, at = group_of(q)
             for c, v in enumerate(cols):
                 h, l0 = c // per_half, (c % per_half) * LANE
-                ag[g][origins[h], h, q * n_dp : (q + 1) * n_dp, l0 : l0 + LANE] = v.astype(BF)
-
-        unpack(recv[k], g, keep)
-        for h, o in enumerate(origins):
-            acc[g][...] += dot(wt[o, h], ag[g][o, h], NT)
+                ag[g][origins[h], h, at, l0 : l0 + LANE] = v.astype(BF)
+
+        unpack(recv[1 + j], slots, keep)
+        for g in range(ng):
+            for h, o in enumerate(origins):
+                acc[g][...] += dot(wt[o, h], ag[g][o, h], NT)
 
     def do_gather(g, hop):
         going = legs(hop + 1) if hop < hops else []
@@ -346,7 +343,8 @@
     def do_hidden(g):
         s0, ns = groups[g]
         cols = slice(s0 * n_dp, (s0 + ns) * n_dp)
-        wait_bytes(ss.at[pl.ds(0, n_t - 1), :, pl.ds(s0 * n_dp, ns * n_dp)], ss_r.at[g])
+        if g == 0:
+            wait_bytes(ss.at[pl.ds(0, n_t - 1)], ss_r)
         total = ss[0, 0:1, cols]
         for j in range(1, n_t):
             total = total + ss[j, 0:1, cols]
@@ -372,10 +370,41 @@
             oacc[g][...] += dot(hid[g][origin], wdb[origin], TN)
 
     def do_back(g):
-        pack(lambda c: oacc[g][:, c * LANE : (c + 1) * LANE], g, send2[g])
+        pack(lambda c: oacc[g][:, c * LANE : (c + 1) * LANE], groups[g][1], send2[g])
         exchange(send2[g], recv2[g], ret_s.at[g], ret_r.at[g])
 
-    does = {"rows": do_rows, "far": do_far, "gather": do_gather, "hidden": do_hidden, "units": do_units, "back": do_back}
+    def do_logits():
+        wait_bytes(lr.at[pl.ds(0, n_t - 1)], lp_r)
+        tot = lr[0]
+        for j in range(1, n_t):
+            tot = tot + lr[j]
+        lg[t] = tot[0] * lax.rsqrt(tot[1] / width + 1e-06)
+
+        def lg_send(i, carry):
+            rcopy(lg.at[t], lg.at[t], lg_s, lg_r, (d, t_peer(i), s)).start()
+            return carry
+
+        lax.fori_loop(1, n_t, lg_send, 0)
+        later(wait_bytes, lg.at[pl.ds(0, n_t - 1)], lg_s)
+
+    def do_weights():
+        r_of = lax.broadcasted_iota(jnp.int32, (experts, rows), 1)
+        expand_t = jnp.where(
+            lax.broadcasted_iota(jnp.int32, (experts, rows), 0) == 2 * (r_of % n_dp) + s, 1.0, 0.0
+        ).astype(BF)
+        slot_of = lax.broadcasted_iota(jnp.int32, (toks, rows), 1) // n_dp + 1
+        mine = dot(taken, expand_t, TN) == slot_of.astype(F32)
+        wait_bytes(lg.at[pl.ds(0, n_t - 1)], lg_r)
+        logits = jnp.concatenate([lg[j] for j in range(n_t)], axis=0).T
+        masked = jnp.where(onehot > 0.0, logits, -jnp.inf)
+        ex = jnp.exp(masked - jnp.max(masked, axis=0, keepdims=True))
+        weights = ex / jnp.sum(ex, axis=0, keepdims=True)
+        w_hi = weights.astype(BF)
+        w_lo = (weights - w_hi.astype(F32)).astype(BF)
+        ct[0] = jnp.where(mine, dot(w_hi, expand_t, TN), 0.0).astype(BF)
+        ct[1] = jnp.where(mine, dot(w_lo, expand_t, TN), 0.0).astype(BF)
+
+    does = {"logits": do_logits, "weights": do_weights, "rows": do_rows, "far": do_far, "farsend": do_farsend, "gather": do_gather, "hidden": do_hidden, "units": do_units, "back": do_back}
     for name, *args in schedule(ng, gather_hops, unit_hops):
         does[name](*args)
 
@@ -386,7 +415,7 @@
             for c, v in enumerate(cols):
                 oacc[g][q * n_dp : (q + 1) * n_dp, c * LANE : (c + 1) * LANE] = v
 
-        unpack(recv2[g], g, keep)
+        unpack(recv2[g], ns, keep)
         for h in range(2):
             z = oacc[g][:, h * feats : (h + 1) * feats].astype(BF)
             cols = slice(s0 * n_dp, (s0 + ns) * n_dp)
@@ -413,6 +442,7 @@
     chunks = 2 * feats // LANE
     n_rows = [ns * n_dp for _, ns in groups]
     planes = [plane_rows(ns, chunks) for _, ns in groups]
+    plane = plane_rows(slots, chunks)
     rows = slots * n_dp
     gather_hops, unit_hops = n_t // 2 - 1, n_t // 2
     piece = toks // n_t
@@ -426,10 +456,12 @@
             vm((2, toks, feats), BF),
             vm((toks, feats), BF),
             vm((2, 2, toks, feats), BF),
+            vm((toks, feats), BF),
+            vm((hid_n, 2 * feats), BF),
             vm((2, feats, experts), BF),
             vm((2, 8, feats), F32),
             vm((rows, toks), BF),
-            vm((n_dp * max(planes), LANE), F32),
+            vm((n_dp * plane, LANE), F32),
             vm((n_t, 2, piece, experts), F32),
             vm((n_t, 2, piece, experts), F32),
             vm((n_t, piece, experts), F32),
@@ -440,15 +472,17 @@
             vm((2, toks, feats), F32),
             vm((toks, feats), F32),
         ]
-        + plane_bufs * 8
+        + [vm((n_dp, plane, LANE), BF)] * 6
+        + plane_bufs * 2
+        + [vm((n_t, hid_n, n), BF) for n in n_rows]
+        + [vm((n, 2 * feats), F32) for n in n_rows]
         + [vm((n_t, 2, n, feats), BF) for n in n_rows]
-        + [vm((n_t, hid_n, n), BF) for n in n_rows]
         + [vm((2 * hid_n, n), F32) for n in n_rows]
-        + [vm((n, 2 * feats), F32) for n in n_rows]
-        + [dma((3,)), dma((3,)), dma((4,)), dma((4,))]
+        + [dma((3,)), dma((3,)), dma((7,)), dma((7,))]
         + [dma] * 10
-        + [dma((3 * ng,))] * 2
-        + [dma((ng,))] * 4
+        + [dma((3,))] * 2
+        + [dma((ng,))] * 2
+        + [dma] * 2
         + [dma((ng, 4 * gather_hops))] * 2
         + [dma((ng, 4 * unit_hops))] * 2
     )

time: 139 us -> 133 us (0.957)
  Pallas kernels: 137 us -> 131 us
    pallas_call x1, Pallas kernels: 137 us -> 131 us  [body(): pl.pallas_call(functools.partial(kernel, cfg), out_shape=jax.ShapeDtypeSt...]
where the time goes in v3:
time: 133 us
  Pallas kernels  131 us (98%)
  local copies, waits for them, and re-layouts  1.47 us (1%)
    pallas_call x1, Pallas kernels, body(): pl.pallas_call(functools.partial(kernel, cfg), out_shape=jax.ShapeDtypeSt...  131 us

profile of v3, /device:TPU:1, one launch (start us, length us, event | category | flops | bytes accessed | tf_op | source)
XLA Modules:
  0.0 132.9 jit_solution(17579289302802816965)
XLA Ops:
  0.0 131.4 %routed_experts.1 = bf16[128,256]{1,0:T(8,128)(2,1)} custom-call(bf16[128,256]{1,0:T(8,128)(2,1)} %refs_0_.1, bf16[256]{0:T(256)(128)(2,1)} %refs_1_.1, bf16[256,128]{1,0:T(8,128)(2,1)} %refs_2_.1, s32[8,128]{1,0:T(8,128)} %bitcast.5, bf16[1,96,4096]{2,1,0:T(8,128)(2,1)} %bitcast.3, bf16[1,96,4096]{2,1,0:T(8,128)(2,1)} %bitcast.4, bf16[1,96,4096]{2,1,0:T(8,128)(2,1)} %refs_6_.1), custom_call_target="tpu_custom_call" | custom-call | tf_op jit(solution)/shard_map/routed_experts/pallas_call | solution.py:490
  131.4 1.5 %copy.9 = bf16[128,256]{1,0:T(8,128)(2,1)} copy(bf16[128,256]{1,0:T(8,128)(2,1)} %routed_experts.1) | data formatting | bytes 131072

commit v4 on v3

--- a/solution.py
+++ b/solution.py
@@ -32,13 +32,15 @@
     steps = [("farsend", 0), ("rows",), ("farsend", 1), ("logits",)]
     for k in range(1, gather_hops):
         steps += [("gather", g, k) for g in range(ng)]
-    steps += [("weights",), ("far", 0), ("far", 1)]
+        if k == 1:
+            steps += [("far", 0)]
+    steps += [("far", 1)] if gather_hops > 1 else [("far", 0), ("far", 1)]
     for g in range(ng):
         steps += [("gather", g, gather_hops), ("hidden", g)]
     for k in range(1, unit_hops + 1):
         for g in range(ng):
             steps += [("units", g, k)] + ([("back", g)] if k == unit_hops else [])
-    return steps
+    return steps + [("weights",)]
 
 
 def kernel(cfg, *refs):

time: 133 us -> 133 us (level)
  no operation moved by 1% of the time
where the time goes in v4:
time: 133 us
  Pallas kernels  131 us (98%)
  local copies, waits for them, and re-layouts  1.47 us (1%)
    pallas_call x1, Pallas kernels, body(): pl.pallas_call(functools.partial(kernel, cfg), out_shape=jax.ShapeDtypeSt...  131 us

profile of v4, /device:TPU:1, one launch (start us, length us, event | category | flops | bytes accessed | tf_op | source)
XLA Modules:
  0.0 132.9 jit_solution(9901812277122791479)
XLA Ops:
  0.0 131.4 %routed_experts.1 = bf16[128,256]{1,0:T(8,128)(2,1)} custom-call(bf16[128,256]{1,0:T(8,128)(2,1)} %refs_0_.1, bf16[256]{0:T(256)(128)(2,1)} %refs_1_.1, bf16[256,128]{1,0:T(8,128)(2,1)} %refs_2_.1, s32[8,128]{1,0:T(8,128)} %bitcast.5, bf16[1,96,4096]{2,1,0:T(8,128)(2,1)} %bitcast.3, bf16[1,96,4096]{2,1,0:T(8,128)(2,1)} %bitcast.4, bf16[1,96,4096]{2,1,0:T(8,128)(2,1)} %refs_6_.1), custom_call_target="tpu_custom_call" | custom-call | tf_op jit(solution)/shard_map/routed_experts/pallas_call | solution.py:492
  131.4 1.5 %copy.9 = bf16[128,256]{1,0:T(8,128)(2,1)} copy(bf16[128,256]{1,0:T(8,128)(2,1)} %routed_experts.1) | data formatting | bytes 131072
